TPU v7x, 256 devices: a whole 4x4x8 slice. The times are simulated.
256 devices in a mesh: tm: 32 (over y, z), chan: 8 (over x, core).
Axes of the slice: x: 4, y: 4, z: 8, core: 2. Of those that a mesh axis runs over, the one named last changes fastest.
Arguments:
- observations: bfloat16 [8192, 8192], P('tm', 'chan'), may hold values from -6 to 6
- emission: bfloat16 [8192, 256], P('chan'), may hold values from -0.0625 to 0.0625
- noise_precision: float32 [8192], P('chan'), may hold values from 0.3 to 3
- transition: float32 [256, 256], replicated, may hold values from -1 to 1
- info_gain: float32 [256, 256], replicated, may hold values from -2 to 2
- smoother_gain: float32 [256, 256], replicated, may hold values from -1 to 1
- smoother_input: float32 [256, 256], replicated, may hold values from -0.1 to 0.1
Outputs:
- smoothed: float32 [8192, 256], P('tm')
- cross_stat: float32 [8192, 256], P('chan')
- noise_var: float32 [8192], P('chan')
- state_moment: float32 [256, 256], replicated
All inputs are finite; a program needn't handle non-finite values.
Results may differ from a plain program's by a relative error of at most 0.0039.
Values sent between devices are 32-bit elements; how exact they have to be, the bound alone decides.
No kernel may reach another device: no remote copies, remote signals or barrier semaphores. Data moves between devices by JAX's collectives and lax.ppermute only.
A program may use at most 256 MiB of HBM per device.

v0:
```python
import math

import jax
import jax.numpy as jnp
from jax import lax
from jax.sharding import PartitionSpec as P

FULL_PRECISION = lax.Precision.HIGHEST


def prefix(part, axis, combine, identity, reverse):
    count = lax.axis_size(axis)
    place = lax.axis_index(axis)
    ahead = count - 1 - place if reverse else place
    gathered = jax.tree.map(lambda a: lax.all_gather(a, axis), part)
    state = jax.tree.map(lambda a, e: jnp.zeros_like(a) + jnp.asarray(e, a.dtype), part, identity)

    def one(lap, state):
        source = count - 1 - lap if reverse else lap
        return combine(
            state, jax.tree.map(lambda a: lax.dynamic_index_in_dim(a, source, 0, False), gathered)
        )

    return lax.fori_loop(0, ahead, one, state)


def product(left, right):
    return jnp.dot(left, right, precision=FULL_PRECISION, preferred_element_type=jnp.float32)


def block_end(rows_in, matrix):
    current = rows_in
    powered = matrix
    while current.shape[0] > 1:
        paired = current.reshape(current.shape[0] // 2, 2, current.shape[1])
        current = paired[:, 1] + product(paired[:, 0], powered.T)
        if current.shape[0] > 1:
            powered = product(powered, powered)
    return current[0]


def forward_prefix(rows_in, matrix):
    current = rows_in
    powered = matrix
    offset = 1
    length = current.shape[0]
    while offset < length:
        moved = product(current[: length - offset], powered.T)
        current = current + jnp.concatenate(
            [jnp.zeros((offset, current.shape[1]), jnp.float32), moved], axis=0
        )
        offset = offset * 2
        if offset < length:
            powered = product(powered, powered)
    return current


def backward_prefix(rows_in, matrix):
    current = rows_in
    powered = matrix
    offset = 1
    length = current.shape[0]
    while offset < length:
        moved = product(current[offset:], powered.T)
        current = current + jnp.concatenate(
            [moved, jnp.zeros((offset, current.shape[1]), jnp.float32)], axis=0
        )
        offset = offset * 2
        if offset < length:
            powered = product(powered, powered)
    return current


def matrix_power(matrix, exponent):
    outcome = jnp.eye(matrix.shape[0], dtype=jnp.float32)
    powered = matrix
    remain = exponent
    while remain > 0:
        if remain % 2 == 1:
            outcome = product(outcome, powered)
        remain = remain // 2
        if remain > 0:
            powered = product(powered, powered)
    return outcome


def compose(earlier, later):
    return (product(later[0], earlier[0]), product(later[0], earlier[1]) + later[1])


def neutral(state_width):
    return (jnp.eye(state_width, dtype=jnp.float32), jnp.zeros((state_width,), jnp.float32))


def filter_pass(drive_rows, transition, carry_in, smoother_input, last_block):
    started = drive_rows.at[0].add(product(transition, carry_in))
    filtered = forward_prefix(started, transition)
    inputs = product(filtered, smoother_input.T)
    final_row = jnp.where(last_block, filtered[-1], inputs[-1])
    return inputs.at[-1].set(final_row)


def smoother_pass(inputs, smoother_gain, carry_in):
    started = inputs.at[-1].add(product(smoother_gain, carry_in))
    return backward_prefix(started, smoother_gain)


def local(
    observations, emission, noise_precision, transition, info_gain, smoother_gain, smoother_input
):
    bin_rows = observations.shape[0]
    state_width = transition.shape[0]
    weighted = (emission.astype(jnp.float32) * noise_precision[:, None]).astype(jnp.bfloat16)
    information = lax.psum(
        jnp.dot(observations, weighted, preferred_element_type=jnp.float32), "chan"
    )
    drive_rows = product(information, info_gain.T)
    last_block = lax.axis_index("tm") == lax.axis_size("tm") - 1
    forward_parts = prefix(
        (matrix_power(transition, bin_rows), block_end(drive_rows, transition)),
        "tm",
        compose,
        neutral(state_width),
        False,
    )
    inputs = filter_pass(drive_rows, transition, forward_parts[1], smoother_input, last_block)
    backward_parts = prefix(
        (matrix_power(smoother_gain, bin_rows), block_end(inputs[::-1], smoother_gain)),
        "tm",
        compose,
        neutral(state_width),
        True,
    )
    smoothed = smoother_pass(inputs, smoother_gain, backward_parts[1])
    states_bf = smoothed.astype(jnp.bfloat16)
    cross_local = lax.dot_general(
        observations, states_bf, (((0,), (0,)), ((), ())), preferred_element_type=jnp.float32
    )
    predicted = lax.dot_general(
        states_bf, emission, (((1,), (1,)), ((), ())), preferred_element_type=jnp.float32
    )
    error_rows = observations.astype(jnp.float32) - predicted
    error_local = jnp.sum(error_rows * error_rows, axis=0)
    moment_local = lax.dot_general(
        smoothed,
        smoothed,
        (((0,), (0,)), ((), ())),
        precision=FULL_PRECISION,
        preferred_element_type=jnp.float32,
    )
    cross_sum, error_sum, moment_sum = lax.psum((cross_local, error_local, moment_local), "tm")
    total_bins = bin_rows * lax.axis_size("tm")
    return (
        smoothed,
        cross_sum / math.sqrt(total_bins),
        error_sum / total_bins,
        moment_sum / total_bins,
    )


def solution(mesh):
    placed = (P("tm", "chan"), P("chan", None), P("chan"), P(), P(), P(), P())
    return jax.shard_map(
        local,
        mesh=mesh,
        in_specs=placed,
        out_specs=(P("tm", None), P("chan", None), P("chan"), P()),
        check_vma=False,
    )
```

profile of v0, /device:TPU:24, one launch (start us, length us, event | category | flops | bytes accessed | tf_op | source)
XLA Modules:
  0.0 433.7 jit_solution(9129201512823289722)
XLA Ops:
  8.1 2.5 convolution_bitcast_fusion.1
  20.0 60.2 %all-reduce.20.cloned.1.call-done = f32[256,256]{0,1:T(8,128)} async-done(((f32[256,256]{0,1:T(8,128)}), f32[256,256]{0,1:T(8,128)}) %all-reduce.20.cloned.1.call-update) | async-done | bytes 262160 | tf_op jit(solution)/shard_map/psum | solution.py:114
  80.2 2.3 fusion.93
  82.6 1.8 reshape.144
  84.4 1.3 fusion.80
  88.4 1.3 convolution_add_fusion.5
  89.7 1.2 convolution_add_fusion.7
  91.0 1.2 convolution_add_fusion.9
  93.3 43.0 %all-gather.4 = f32[32,1,256]{2,1,0:T(1,128)S(1)} all-gather(f32[1,1,256]{2,1,0:T(1,128)S(1)} %bitcast.261), channel_id=3, replica_groups=mesh['tm'=32,'chan'=8] {'tm'}, dimensions={0}, use_global_device_ids=true | all-gather | bytes 33792 | tf_op jit(solution)/shard_map/all_gather | solution.py:15
  136.3 32.0 %while.29 = (s32[]{:T(128)}, f32[256]{0:T(256)S(1)}, s32[]{:T(128)}, f32[32,256,256]{2,1,0:T(8,128)}, f32[32,256]{1,0:T(8,128)S(1)}, /*index=5*/s32[]{:T(128)}, s32[]{:T(128)}, s32[]{:T(128)}) while((s32[]{:T(128)}, f32[256]{0:T(256)S(1)}, s32[]{:T(128)}, f32[32,256,256]{2,1,0:T(8,128)}, f32[32,256]{1,0:T(8,128)S(1)}, /*index=5*/s32[]{:T(128)}, ...), condition=%wide.region_2.3_spmd, body=%wide.region_1.2_spmd.sunk | while | flops 786693 | bytes 269439 | solution.py:24
  136.3 1.2 fusion.201
  139.0 1.2 fusion.201
  140.3 1.3 fusion.201
  143.0 1.2 fusion.201
  148.3 1.2 fusion.201
  151.0 1.2 fusion.201
  153.6 1.2 fusion.201
  165.6 1.3 fusion.201
  169.3 1.4 scatter-add.6
  170.7 1.4 fusion.23
  173.6 1.4 fusion.19
  175.0 1.4 fusion.29
  176.4 1.4 fusion.33
  183.4 50.4 %all-gather.5 = f32[32,1,256]{2,1,0:T(1,128)S(1)} all-gather(f32[1,1,256]{2,1,0:T(1,128)S(1)} %bitcast.262), channel_id=5, replica_groups=mesh['tm'=32,'chan'=8] {'tm'}, dimensions={0}, use_global_device_ids=true | all-gather | bytes 33792 | tf_op jit(solution)/shard_map/all_gather | solution.py:15
  233.8 9.3 %while.30 = (s32[]{:T(128)}, f32[256]{0:T(256)S(1)}, s32[]{:T(128)}, f32[32,256,256]{2,1,0:T(8,128)}, f32[32,256]{1,0:T(8,128)S(1)}, /*index=5*/s32[]{:T(128)}, s32[]{:T(128)}, s32[]{:T(128)}, s32[]{:T(128)}) while((s32[]{:T(128)}, f32[256]{0:T(256)S(1)}, s32[]{:T(128)}, f32[32,256,256]{2,1,0:T(8,128)}, f32[32,256]{1,0:T(8,128)S(1)}, ...), condition=%wide.region_4.5_spmd, body=%wide.region_3.4_spmd.sunk | while | flops 786694 | bytes 269459 | solution.py:24
  247.2 1.3 convolution_bitcast_fusion
  248.5 1.3 fusion.111
  250.2 88.7 %psum.30 = f32[1024]{0:T(1024)S(1)} all-reduce(f32[1024]{0:T(1024)S(1)} %fusion.9), channel_id=1, replica_groups=mesh['tm'=32,'chan'=8] {'tm'}, use_global_device_ids=true, to_apply=%region_7.8 | all-reduce | flops 1024 | bytes 8192 | tf_op jit(solution)/shard_map/psum | solution.py:151
  339.4 82.4 %all-reduce.22.cloned.1.call-done = (f32[1024,256]{0,1:T(8,128)}, f32[256,256]{1,0:T(8,128)}) async-done(((f32[1024,256]{0,1:T(8,128)}, f32[256,256]{1,0:T(8,128)}), (f32[1024,256]{0,1:T(8,128)}, f32[256,256]{1,0:T(8,128)})) %all-reduce.22.cloned.1.call-update) | async-done | bytes 1310736 | tf_op jit(solution)/shard_map/psum | solution.py:151
  421.8 1.3 broadcast_multiply_fusion
  423.1 1.3 copy.40
  424.4 1.7 broadcast_multiply_fusion.1
  (215 shorter events, 55.8 us)
Async XLA Ops:
  8.0 2.6 copy-start
  8.0 7.8 %copy-start.1 = (f32[256,256]{1,0:T(8,128)S(1)}, f32[256,256]{1,0:T(8,128)}, u32[]{:S(2)}) copy-start(f32[256,256]{1,0:T(8,128)} %param.22) | copy-start | bytes 786436
  8.0 72.2 %all-reduce.20.cloned.1.call-start = ((), (), s32[]{:S(2)}) async-start(), calls=%async_computation | async-start | bytes 524288 | tf_op jit(solution)/shard_map/psum | solution.py:114
  10.6 125.7 %all-gather.9.cloned.1.call-start = ((), (), s32[]{:S(2)}) async-start(), calls=%async_computation.1 | async-start | bytes 8650752 | tf_op jit(solution)/shard_map/all_gather | solution.py:15
  11.4 0.7 copy-start.4
  12.5 1.5 copy-start.3
  12.9 0.7 copy-start.2
  15.8 218.0 %all-gather.11.cloned.1.call-start = ((), (), s32[]{:S(2)}) async-start(), calls=%async_computation.2 | async-start | bytes 8650752 | tf_op jit(solution)/shard_map/all_gather | solution.py:15
  20.0 401.8 %all-reduce.22.cloned.1.call-start = ((), (), s32[]{:S(2)}) async-start(), calls=%async_computation.3 | async-start | bytes 2621440 | tf_op jit(solution)/shard_map/psum | solution.py:151
  170.7 8.5 %copy-start.7 = (f32[256,256]{1,0:T(8,128)S(1)}, f32[256,256]{1,0:T(8,128)}, u32[]{:S(2)}) copy-start(f32[256,256]{1,0:T(8,128)} %param.23) | copy-start | bytes 786436
  180.7 66.4 %copy-start.6 = (bf16[256,1024]{1,0:T(8,128)(2,1)S(1)}, bf16[256,1024]{1,0:T(8,128)(2,1)}, u32[]{:S(2)}) copy-start(bf16[256,1024]{1,0:T(8,128)(2,1)} %param.17) | copy-start | bytes 1572868
  244.3 5.5 %copy-start.8 = (bf16[1024,256]{1,0:T(8,128)(2,1)S(1)}, bf16[1024,256]{1,0:T(8,128)(2,1)}, u32[]{:S(2)}) copy-start(bf16[1024,256]{1,0:T(8,128)(2,1)} %param.18) | copy-start | bytes 1572868
  247.2 178.9 %copy-start.5 = (f32[256,256]{1,0:T(8,128)}, f32[256,256]{1,0:T(8,128)S(1)}, u32[]{:S(2)}) copy-start(f32[256,256]{1,0:T(8,128)S(1)} %pad_add_fusion) | copy-start | bytes 786436
Sparse Core Ops, SparseCore 0:
  11.7 68.4 all-reduce.19
Sparse Core Ops, SparseCore 1:
  15.9 99.1 all-gather.8
  117.9 95.5 all-gather.10
  249.9 171.8 all-reduce.21
where the time goes:
time: 438 us; the launch traced here: 434 us
  blocking collectives  182 us (42%)
  waiting for transfers between devices  143 us (33%)
  matrix products  73.7 us (17%)
  between operations  16.5 us (4%)
  local copies, waits for them, and re-layouts  12 us (3%)
  other arithmetic  5.25 us (1%)
    all_gather x2, blocking collectives, prefix(): gathered = jax.tree.map(lambda a: lax.all_gather(a, axis), part)  93.3 us
    psum x1, blocking collectives, local(): lax.psum((cross_local, error_local, moment_local), 'tm')  88.7 us
    psum x1, waiting for transfers between devices, local(): lax.psum((cross_local, error_local, moment_local), 'tm')  82.4 us
    dot_general x85, matrix products, product(): jnp.dot(left, right, precision=FULL_PRECISION, preferred_element_type=jnp...  68.3 us
    psum x1, waiting for transfers between devices, local(): lax.psum(jnp.dot(observations, weighted, preferred_element_type=jnp.float...  60.2 us
  transfers between devices with their start and end apart: 4, of which 2 were waited for; matrix products, arithmetic and copies ran while one was open for 16% of the time, Pallas kernels for 0%

commit v1 on v0

v1 whole, which is shorter than its diff:
```python
import functools
import math

import jax
import jax.numpy as jnp
import numpy as np
from jax import lax
from jax.experimental import pallas as pl
from jax.experimental.pallas import tpu as pltpu
from jax.sharding import Mesh, PartitionSpec as P

N_Y, N_Z, N_X, N_CORE = 4, 8, 4, 2
BLOCKS = N_Y * N_Z
SUB = 8
F32, BF16 = jnp.float32, jnp.bfloat16
KERNELS = True


def call(body, outs, *args):
    if not KERNELS:
        return body(*args)

    def kernel(*refs):
        values = body(*[ref[...] for ref in refs[: len(args)]])
        for ref, value in zip(refs[len(args) :], values):
            ref[...] = value

    return pl.pallas_call(
        kernel,
        out_shape=[jax.ShapeDtypeStruct(shape, dtype) for shape, dtype in outs],
        compiler_params=pltpu.CompilerParams(vmem_limit_bytes=56 * 2**20),
        name=body.__name__,
    )(*args)


def roll(rows, by):
    if KERNELS:
        return pltpu.roll(rows, by % rows.shape[0], 0)
    return jnp.roll(rows, by, 0)


def row_index(rows):
    return lax.broadcasted_iota(jnp.int32, rows.shape, 0)


def dot(left, right, dims=((1,), (0,))):
    return lax.dot_general(left, right, (dims, ((), ())), preferred_element_type=F32)


def dot_full(left, right):
    return jnp.dot(left, right, precision=lax.Precision.HIGHEST, preferred_element_type=F32)


def cut(value):
    high = value.astype(BF16)
    return high, (value - high.astype(F32)).astype(BF16)


def mul(rows, high, low):
    rows_high, rows_low = cut(rows)
    return dot(rows_high, high) + (dot(rows_low, high) + dot(rows_high, low))


def stack_cut(values):
    pairs = [cut(value) for value in values]
    return jnp.stack([p[0] for p in pairs]), jnp.stack([p[1] for p in pairs])


def small_powers(transition, info_gain, smoother_gain, smoother_input):
    a, b, g, k = transition.T, smoother_gain.T, smoother_input.T, info_gain.T
    kg = dot_full(k, g)
    ag = dot_full(a, g)
    lead = stack_cut([k, kg, dot_full(kg, b), ag, g])
    m = dot_full(ag, b)
    a_list, b_list, m_list, n_list = [], [], [], []
    for _ in range(8):
        a_list.append(a)
        b_list.append(b)
        m_list.append(m)
        n = mul(a, *cut(m))
        n_list.append(n)
        m = m + mul(n, *cut(b))
        a, b = dot_full(a, a), dot_full(b, b)
    return (
        *lead,
        *stack_cut(a_list),
        *stack_cut(b_list),
        *stack_cut(m_list),
        *stack_cut(n_list),
        a,
        b,
        m,
    )


def big_powers(a, b, m):
    a_list, b_list = [a], [b]
    for _ in range(4):
        a_list.append(dot_full(a_list[-1], a_list[-1]))
        b_list.append(dot_full(b_list[-1], b_list[-1]))
    return (*stack_cut(a_list), *stack_cut(b_list), *cut(m))


def information_part(core, order, observations, emission, noise_precision):
    rows = dot(order, observations).astype(BF16)
    scale = jnp.broadcast_to(noise_precision, (128, noise_precision.shape[1])).T
    scale = jnp.concatenate([scale] * (emission.shape[1] // 128), axis=1)
    weighted = (emission.astype(F32) * scale).astype(BF16)
    information = dot(rows, weighted)
    half = rows.shape[0] // 2
    first = jnp.broadcast_to(core, (half, information.shape[1])) == 0
    mine = jnp.where(first, information[:half], information[half:])
    other = jnp.where(first, information[half:], information[:half])
    return mine, other


def channel_slices(order, observations):
    rows = dot(order, observations)
    width = rows.shape[1] // N_Y
    return tuple(rows[:, i * width : (i + 1) * width] for i in range(N_Y))


def up_sweep(lead, a_cut, b_cut, m_cut, information):
    lead_high, lead_low = lead
    drive = mul(information, lead_high[0], lead_low[0])
    shown = mul(information, lead_high[1], lead_low[1])
    end = drive
    start = mul(information, lead_high[2], lead_low[2])
    ends, follows = [], []
    for level in range(5):
        half = end.shape[0] // 2
        first, second = end[:half], end[half:]
        follow = start[half:] + mul(first, m_cut[0][level], m_cut[1][level])
        ends.append(first)
        follows.append(follow)
        start = start[:half] + mul(follow, b_cut[0][level], b_cut[1][level])
        end = second + mul(first, a_cut[0][level], a_cut[1][level])
    return shown, end, start, ends, follows


def sub_sweep(a_cut, b_cut, m_cut, end, start):
    ends, follows = [], []
    for level in range(5, 8):
        by = 2 ** (level - 5)
        follow = roll(start, -by) + mul(end, m_cut[0][level], m_cut[1][level])
        ends.append(end)
        follows.append(follow)
        start = start + mul(follow, b_cut[0][level], b_cut[1][level])
        end = mul(end, a_cut[0][level], a_cut[1][level]) + roll(end, -by)
    return end, start, ends, follows


def block_ends(core, total, theirs, lead_h, lead_l, a_h, a_l, b_h, b_l, m_h, m_l):
    first = jnp.broadcast_to(core, total.shape) == 0
    information = jnp.concatenate(
        [jnp.where(first, total, theirs), jnp.where(first, theirs, total)], axis=0
    )
    a_cut, b_cut, m_cut = (a_h, a_l), (b_h, b_l), (m_h, m_l)
    _, end, start, _, _ = up_sweep((lead_h, lead_l), a_cut, b_cut, m_cut, information)
    end, start, _, _ = sub_sweep(a_cut, b_cut, m_cut, end, start)
    pair = jnp.concatenate([end[None, :1], start[None, :1]], axis=1)
    return information, jnp.broadcast_to(pair, (BLOCKS, 2, end.shape[1]))


def spread_first(rows, by):
    rows = jnp.where(row_index(rows) % (2 * by) == 0, rows, 0.0)
    step = 1
    while step < 2 * by:
        rows = rows + roll(rows, step)
        step *= 2
    return rows


def joined(pieces):
    width = pieces[0].shape[1]
    return jnp.concatenate(
        [piece.reshape(-1, 1, SUB, width) for piece in pieces], axis=1
    ).reshape(-1, width)


def block_trees(
    o0, o1, o2, o3, i0, i1, i2, i3, lead_h, lead_l, a_h, a_l, b_h, b_l, m_h, m_l
):
    a_cut, b_cut, m_cut = (a_h, a_l), (b_h, b_l), (m_h, m_l)
    information = joined([i0, i1, i2, i3])
    shown, end, start, ends, follows = up_sweep(
        (lead_h, lead_l), a_cut, b_cut, m_cut, information
    )
    _, _, sub_ends, sub_follows = sub_sweep(a_cut, b_cut, m_cut, end, start)
    sub_ends = [spread_first(rows, 2**i) for i, rows in enumerate(sub_ends)]
    sub_follows = [spread_first(rows, 2**i) for i, rows in enumerate(sub_follows)]
    observed = joined([o0, o1, o2, o3]).astype(BF16)
    return (
        shown,
        jnp.concatenate(ends, axis=0),
        jnp.concatenate(follows, axis=0),
        jnp.concatenate(sub_ends, axis=0),
        jnp.concatenate(sub_follows, axis=0),
        observed,
    )


def states_and_sums(
    block,
    natural,
    gathered,
    shown,
    ends,
    follows,
    sub_ends,
    sub_follows,
    observed,
    emission,
    lead_h,
    lead_l,
    a_h,
    a_l,
    b_h,
    b_l,
    n_h,
    n_l,
    a_big_h,
    a_big_l,
    b_big_h,
    b_big_l,
    m_h,
    m_l,
):
    width = shown.shape[1]
    after = gathered[:, 0]
    index = row_index(after)
    for level in range(5):
        by = 2**level
        before = jnp.where(index >= by, roll(after, by), 0.0)
        after = after + mul(before, a_big_h[level], a_big_l[level])
    enter = jnp.where(index >= 1, roll(after, 1), 0.0)
    follow = gathered[:, 1] + mul(enter, m_h, m_l)
    final = after - mul(after, lead_h[4], lead_l[4])
    follow = jnp.where(index < BLOCKS - 1, roll(follow, -1), final)
    for level in range(5):
        by = 2**level
        later = jnp.where(index < BLOCKS - by, roll(follow, -by), 0.0)
        follow = follow + mul(later, b_big_h[level], b_big_l[level])

    place = lax.broadcasted_iota(jnp.int32, (N_Y * SUB, BLOCKS), 0)
    source = lax.broadcasted_iota(jnp.int32, (N_Y * SUB, BLOCKS), 1)
    wanted = jnp.broadcast_to(block, place.shape) - N_Z * (place // SUB)
    pick = (source == jnp.where(wanted < 0, wanted + BLOCKS, wanted)).astype(BF16)

    def picked(rows):
        high, low = cut(rows)
        return dot(pick, high) + dot(pick, low)

    enter, follow = picked(enter), picked(follow)
    count = N_Y * SUB
    index = row_index(enter)
    for level in (7, 6, 5):
        by = 2 ** (level - 5)
        part = (level - 5) * count
        second = sub_ends[part : part + count] + mul(enter, a_h[level], a_l[level])
        first = (
            sub_follows[part : part + count]
            + mul(enter, n_h[level], n_l[level])
            + mul(follow, b_h[level], b_l[level])
        )
        is_second = (index // by) % 2 == 1
        enter = jnp.where(is_second, second, enter)
        follow = jnp.where(is_second, follow, first)

    bottom = ends.shape[0]
    for level in (4, 3, 2, 1, 0):
        rows = enter.shape[0]
        top, bottom = bottom, bottom - rows
        second = ends[bottom:top] + mul(enter, a_h[level], a_l[level])
        first = (
            follows[bottom:top]
            + mul(enter, n_h[level], n_l[level])
            + mul(follow, b_h[level], b_l[level])
        )
        enter = jnp.concatenate([enter, second], axis=0)
        follow = jnp.concatenate([first, follow], axis=0)
    smoothed = shown + mul(enter, lead_h[3], lead_l[3]) + follow

    high, low = cut(smoothed)
    cross = dot(observed, high, ((0,), (0,)))
    predicted = dot(high, emission, ((1,), (1,)))
    error = observed.astype(F32) - predicted
    error = jnp.broadcast_to(jnp.sum(error * error, axis=0, keepdims=True), (8, error.shape[1]))
    crossed = dot(high, jnp.concatenate([high, low], axis=1), ((0,), (0,)))
    moment = crossed[:, :width] + (crossed[:, width:] + crossed[:, width:].T)

    own = smoothed.reshape(-1, N_Y, SUB, width)[:, 0].reshape(-1, width)
    high, rest = own.astype(BF16), own
    out = dot(natural, high)
    for _ in range(2):
        rest = rest - high.astype(F32)
        high = rest.astype(BF16)
        out = out + dot(natural, high)

    channels = cross.shape[0]
    share = moment.shape[0] // N_Y
    y = jnp.broadcast_to(block, (share, width)) // N_Z
    mine = moment[:share]
    for i in range(1, N_Y):
        mine = jnp.where(y == i, moment[i * share : (i + 1) * share], mine)
    payload = jnp.concatenate(
        [
            cross.reshape(N_Z, channels // N_Z, width),
            mine.reshape(N_Z, share // N_Z, width),
            jnp.broadcast_to(error[None], (N_Z,) + error.shape),
        ],
        axis=1,
    )
    return out, payload


def add_pieces(pieces):
    total = pieces[0]
    for i in range(1, N_Z):
        total = total + pieces[i]
    kept = total.shape[0] - 8
    return jnp.broadcast_to(total[None, :kept], (N_Z, kept, total.shape[1])), total[kept:]


def assemble(bins, channel_rows, place, sums, errors):
    width = sums[0].shape[2]
    cross, moment, error = [], [], []
    for i in range(N_Y):
        want = jnp.broadcast_to(place, sums[0].shape) - i
        want = jnp.where(want < 0, want + N_Y, want)
        whole = sums[0]
        for by in range(1, N_Y):
            whole = jnp.where(want == by, sums[by], whole)
        cross.append(whole[:, :channel_rows].reshape(-1, width) * (1.0 / math.sqrt(bins)))
        moment.append(whole[:, channel_rows:].reshape(-1, width) * (1.0 / bins))
        want = want[0, :8]
        line = errors[0]
        for by in range(1, N_Y):
            line = jnp.where(want == by, errors[by], line)
        error.append(line[:1] * (1.0 / bins))
    return (
        jnp.concatenate(cross, axis=0),
        jnp.concatenate(moment, axis=0),
        jnp.concatenate(error, axis=1),
    )


def shift(value, axis, count, by):
    return lax.ppermute(value, axis, [(i, (i + by) % count) for i in range(count)])


def bit_reversed(count):
    bits = count.bit_length() - 1
    return [int(format(i, "0%db" % bits)[::-1], 2) for i in range(count)]


def row_order(bins):
    length = bins // SUB
    times = np.array([[j * length + t for j in range(SUB)] for t in bit_reversed(length)])
    return np.eye(bins, dtype=np.float32)[times.reshape(-1)]


def local(
    observations, emission, noise_precision, transition, info_gain, smoother_gain, smoother_input
):
    bins, channels = observations.shape
    width = transition.shape[0]
    y, core = lax.axis_index("y"), lax.axis_index("core")
    order = jnp.asarray(row_order(bins), BF16)
    natural = jnp.asarray(row_order(bins).T, BF16)
    one = lambda number: number.astype(jnp.int32).reshape(1, 1)

    mine, other = call(
        information_part,
        [((bins // 2, width), F32)] * 2,
        one(core),
        order,
        observations,
        emission,
        noise_precision.reshape(1, channels),
    )
    mine = mine + shift(other, "core", N_CORE, 1)
    moved = [shift(mine, "x", N_X, by) for by in (2, 1, 3)]

    slices = call(channel_slices, [((bins, channels // N_Y), F32)] * N_Y, order, observations)
    slices = jnp.stack(slices)
    piece = lambda by: lax.dynamic_index_in_dim(slices, (y + by) % N_Y, 0, False)
    observed = [piece(0)] + [shift(piece(by), "y", N_Y, by) for by in (1, 2, 3)]
    emission_part = lax.dynamic_slice_in_dim(
        emission, y * (channels // N_Y), channels // N_Y, 0
    )

    square = (width, width)
    stack = lambda n: [((n,) + square, BF16)] * 2
    small = call(
        small_powers,
        stack(5) + stack(8) * 4 + [(square, F32)] * 3,
        transition,
        info_gain,
        smoother_gain,
        smoother_input,
    )
    lead, a_cut, b_cut, m_cut, n_cut = (small[i : i + 2] for i in range(0, 10, 2))

    total = mine + moved[0] + moved[1] + moved[2]
    theirs = shift(total, "core", N_CORE, 1)
    information, ends = call(
        block_ends,
        [((bins, width), F32), ((BLOCKS, 2, width), F32)],
        one(core),
        total,
        theirs,
        *lead,
        *a_cut,
        *b_cut,
        *m_cut,
    )
    gathered = lax.all_to_all(ends, ("y", "z"), 0, 0)
    informations = [information] + [shift(information, "y", N_Y, by) for by in (1, 2, 3)]
    big = call(big_powers, stack(5) * 2 + [(square, BF16)] * 2, *small[10:])
    tree_rows = N_Y * SUB * 31
    shown, tree_ends, follows, sub_ends, sub_follows, seen = call(
        block_trees,
        [
            ((N_Y * bins, width), F32),
            ((tree_rows, width), F32),
            ((tree_rows, width), F32),
            ((3 * N_Y * SUB, width), F32),
            ((3 * N_Y * SUB, width), F32),
            ((N_Y * bins, channels // N_Y), BF16),
        ],
        *observed,
        *informations,
        *lead,
        *a_cut,
        *b_cut,
        *m_cut,
    )
    channel_rows, moment_rows = channels // (N_Y * N_Z), width // (N_Y * N_Z)
    smoothed, payload = call(
        states_and_sums,
        [((bins, width), F32), ((N_Z, channel_rows + moment_rows + 8, width), F32)],
        one(lax.axis_index(("y", "z"))),
        natural,
        gathered,
        shown,
        tree_ends,
        follows,
        sub_ends,
        sub_follows,
        seen,
        emission_part,
        *lead,
        *a_cut,
        *b_cut,
        *n_cut,
        *big,
    )
    payload = lax.all_to_all(payload, "z", 0, 0)
    spread, error = call(
        add_pieces,
        [((N_Z, channel_rows + moment_rows, width), F32), ((8, width), F32)],
        payload,
    )
    whole = lax.all_to_all(spread, "z", 0, 0)
    errors = [error] + [shift(error, "y", N_Y, by) for by in (1, 2, 3)]
    sums = [whole] + [shift(whole, "y", N_Y, by) for by in (2, 1, 3)]
    sums = [sums[0], sums[2], sums[1], sums[3]]

    def finish(place, s0, s1, s2, s3, e0, e1, e2, e3):
        return assemble(bins * BLOCKS, channel_rows, place, [s0, s1, s2, s3], [e0, e1, e2, e3])

    cross, moment, error = call(
        finish,
        [((channels, width), F32), (square, F32), ((1, channels), F32)],
        one(y),
        *sums,
        *errors,
    )
    return smoothed, cross, error.reshape(channels), moment


def solution(mesh):
    tm, chan = ("y", "z"), ("x", "core")
    split = Mesh(mesh.devices.reshape(N_Y, N_Z, N_X, N_CORE), tm + chan)
    placed = (P(tm, chan), P(chan, None), P(chan), P(), P(), P(), P())
    return jax.shard_map(
        local,
        mesh=split,
        in_specs=placed,
        out_specs=(P(tm, None), P(chan, None), P(chan), P()),
        check_vma=False,
    )
```

time: 438 us -> 147 us (0.34)
  blocking collectives: 182 us -> 34.7 us
  waiting for transfers between devices: 143 us -> 17.4 us
  matrix products: 73.7 us -> 0 us
  Pallas kernels: 0 us -> 55.9 us
  starting transfers between devices: 0.17 us -> 30.4 us
  between operations: 16.5 us -> 0.87 us
  local copies, waits for them, and re-layouts: 12 us -> 5.58 us
    psum x2 -> x0, waiting for transfers between devices: 143 us -> none  [the longest x1 82.4 us: local(): lax.psum((cross_local, error_local, moment_local), 'tm')]
    all_gather x2 -> x0, blocking collectives: 93.3 us -> none  [prefix(): gathered = jax.tree.map(lambda a: lax.all_gather(a, axis), part)]
    psum x1 -> x0, blocking collectives: 88.7 us -> none  [local(): lax.psum((cross_local, error_local, moment_local), 'tm')]
    dot_general x89 -> x0, matrix products: 73.7 us -> none  [the longest x85 68.3 us: product(): jnp.dot(left, right, precision=FULL_PRECISION, preferred_element_type=jnp...]
    pallas_call x0 -> x9, Pallas kernels: none -> 55.9 us  [call(): pl.pallas_call(kernel, out_shape=[jax.ShapeDtypeStruct(shape, dtype) for...]
    all_to_all x0 -> x2, blocking collectives: none -> 34.7 us  [the longest x1 20.1 us: local(): payload = lax.all_to_all(payload, 'z', 0, 0)]
    ppermute x0 -> x17, starting transfers between devices: none -> 18 us  [shift(): lax.ppermute(value, axis, [(i, (i + by) % count) for i in range(count)])]
    ppermute x0 -> x17, waiting for transfers between devices: none -> 17.4 us  [shift(): lax.ppermute(value, axis, [(i, (i + by) % count) for i in range(count)])]
  transfers between devices with their start and end apart: 4 -> 18, of which waited for: 2 -> 5; matrix products, arithmetic and copies ran while one was open for 16% -> 3% of each run, Pallas kernels for 0% -> 25%
where the time goes in v1:
time: 147 us; the launch traced here: 146 us
  Pallas kernels  55.9 us (38%)
  blocking collectives  34.7 us (24%)
  starting transfers between devices  30.4 us (21%)
  waiting for transfers between devices  17.4 us (12%)
  local copies, waits for them, and re-layouts  5.58 us (4%)
    pallas_call x9, Pallas kernels, call(): pl.pallas_call(kernel, out_shape=[jax.ShapeDtypeStruct(shape, dtype) for...  55.9 us
    all_to_all x1, blocking collectives, local(): payload = lax.all_to_all(payload, 'z', 0, 0)  20.1 us
    ppermute x17, starting transfers between devices, shift(): lax.ppermute(value, axis, [(i, (i + by) % count) for i in range(count)])  18 us
    ppermute x17, waiting for transfers between devices, shift(): lax.ppermute(value, axis, [(i, (i + by) % count) for i in range(count)])  17.4 us
    all_to_all x1, blocking collectives, local(): whole = lax.all_to_all(spread, 'z', 0, 0)  14.6 us
    all_to_all x1, starting transfers between devices, local(): gathered = lax.all_to_all(ends, ('y', 'z'), 0, 0)  12.4 us
    unnamed x36, local copies, waits for them, and re-layouts  3.24 us
  transfers between devices with their start and end apart: 18, of which 5 were waited for; matrix products, arithmetic and copies ran while one was open for 3% of the time, Pallas kernels for 25%

profile of v1, /device:TPU:24, one launch (start us, length us, event | category | flops | bytes accessed | tf_op | source)
XLA Modules:
  0.0 146.3 jit_solution(4412999803432174662)
XLA Ops:
  0.6 2.5 %information_part.1 = (f32[128,256]{1,0:T(8,128)}, f32[128,256]{1,0:T(8,128)}) custom-call(s32[1,1]{1,0:T(1,128)} %bitcast.1.refs_0_, bf16[256,256]{1,0:T(8,128)(2,1)} %constant.65.clone.refs_1_.refs_0_, bf16[256,1024]{1,0:T(8,128)(2,1)} %refs_1_.5, bf16[1024,256]{1,0:T(8,128)(2,1)} %refs_3_.2, f32[1,1024]{1,0:T(1,128)} %bitcast.21), custom_call_target="tpu_custom_call" | custom-call | tf_op jit(solution)/shard_map/information_part/pallas_call | solution.py:28
  3.1 2.3 %channel_slices.1 = (f32[256,256]{1,0:T(8,128)}, f32[256,256]{1,0:T(8,128)}, f32[256,256]{1,0:T(8,128)}, f32[256,256]{1,0:T(8,128)}) custom-call(bf16[256,256]{1,0:T(8,128)(2,1)} %constant.65.clone.refs_1_.refs_0_, bf16[256,1024]{1,0:T(8,128)(2,1)} %refs_1_.5), custom_call_target="tpu_custom_call" | custom-call | tf_op jit(solution)/shard_map/channel_slices/pallas_call | solution.py:28
  5.5 1.3 pad_maximum_fusion
  6.8 2.8 %collective-permute-start.3 = (f32[128,256]{1,0:T(8,128)S(1)}, f32[128,256]{1,0:T(8,128)S(1)}, u32[]{:S(2)}, u32[]{:S(2)}) collective-permute-start(f32[128,256]{1,0:T(8,128)S(1)} %add.54), channel_id=1, source_target_pairs={{0,6},{2,0},{4,2},{6,4},{1,7},{3,1},{5,3},{7,5},{8,14},{10,8},{12,... | collective-permute-start | bytes 393224 | tf_op jit(solution)/shard_map/ppermute | solution.py:349
  9.7 2.3 %collective-permute-start.1 = (f32[128,256]{1,0:T(8,128)S(1)}, f32[128,256]{1,0:T(8,128)S(1)}, u32[]{:S(2)}, u32[]{:S(2)}) collective-permute-start(f32[128,256]{1,0:T(8,128)S(1)} %add.54), channel_id=1, source_target_pairs={{0,4},{2,6},{4,0},{6,2},{1,5},{3,7},{5,1},{7,3},{8,12},{10,14},{12... | collective-permute-start | bytes 393224 | tf_op jit(solution)/shard_map/ppermute | solution.py:349
  12.0 0.8 dynamic-slice_bitcast_fusion
  13.1 6.2 %collective-permute-done.2 = f32[128,256]{1,0:T(8,128)S(1)} collective-permute-done((f32[128,256]{1,0:T(8,128)S(1)}, f32[128,256]{1,0:T(8,128)S(1)}, u32[]{:S(2)}, u32[]{:S(2)}) %collective-permute-start.2) | collective-permute-done | bytes 131104 | tf_op jit(solution)/shard_map/ppermute | solution.py:349
  19.5 1.3 collective-permute-start.6
  20.8 11.2 %small_powers.1 = (bf16[5,256,256]{2,1,0:T(8,128)(2,1)}, bf16[5,256,256]{2,1,0:T(8,128)(2,1)}, bf16[8,256,256]{2,1,0:T(8,128)(2,1)}, bf16[8,256,256]{2,1,0:T(8,1...) custom-call(f32[256,256]{1,0:T(8,128)} %refs_0_.2, ...), custom_call_target="tpu_custom_call" | custom-call | tf_op jit(solution)/shard_map/small_powers/pallas_call | solution.py:28
  32.0 0.6 copy-done.12
  32.6 6.9 %block_ends.1 = (f32[256,256]{1,0:T(8,128)}, f32[32,2,256]{2,1,0:T(2,128)}) custom-call(s32[1,1]{1,0:T(1,128)} %bitcast.1.refs_0_, f32[128,256]{1,0:T(8,128)} %copy-done.1, f32[128,256]{1,0:T(8,128)} %copy-done.12, bf16[5,256,256]{2,1,0:T(8,128)(2,1)} %get-tuple-element.46.refs_3_.refs_8_.refs_10_, ...), custom_call_target="tpu_custom_call" | custom-call | tf_op jit(solution)/shard_map/block_ends/pallas_call | solution.py:28
  39.6 3.2 %collective-permute-start.8 = (f32[256,256]{1,0:T(8,128)}, f32[256,256]{1,0:T(8,128)S(1)}, u32[]{:S(2)}, u32[]{:S(2)}) collective-permute-start(f32[256,256]{1,0:T(8,128)} %get-tuple-element.59.refs_4_), channel_id=1, source_target_pairs={{0,64},{64,128},{128,192},{192,0},{1,65},{65,129},{129,193},{193,1... | collective-permute-start | bytes 786440 | tf_op jit(solution)/shard_map/ppermute | solution.py:349
  42.8 1.1 collective-permute-start.9
  43.9 0.7 collective-permute-start.10
  44.6 12.4 %all-to-all-start = ((f32[32,2,256]{2,1,0:T(2,128)}), f32[32,2,256]{2,1,0:T(2,128)S(1)}, u32[]{:S(2)}, u32[]{:S(2)}) async-start(f32[32,2,256]{2,1,0:T(2,128)} %get-tuple-element.54), calls=%async_computation | async-start | bytes 131072 | tf_op jit(solution)/shard_map/all_to_all | solution.py:418
  57.1 5.2 %big_powers.1 = (bf16[5,256,256]{2,1,0:T(8,128)(2,1)}, bf16[5,256,256]{2,1,0:T(8,128)(2,1)}, bf16[5,256,256]{2,1,0:T(8,128)(2,1)}, bf16[5,256,256]{2,1,0:T(8,128...) custom-call(f32[256,256]{1,0:T(8,128)} %get-tuple-element.68.refs_0_, f32[256,256]{1,0:T(8,128)} %get-tuple-element.69.refs_1_, ...), custom_call_target="tpu_custom_call" | custom-call | tf_op jit(solution)/shard_map/big_powers/pallas_call | solution.py:28
  62.3 1.6 %constant_dynamic-slice_fusion.refs_9_ = bf16[256,256]{1,0:T(8,128)(2,1)} fusion(bf16[1024,256]{1,0:T(8,128)(2,1)} %refs_3_.2, s32[]{:T(128)S(6)} %select_n.43), kind=kLoop, calls=%fused_computation.6 | loop fusion | bytes 262148 | tf_op jit(solution)/shard_map/dynamic_slice | solution.py:389
  63.9 0.6 copy-done.7
  64.9 10.9 %block_trees.1 = (f32[1024,256]{1,0:T(8,128)}, f32[992,256]{1,0:T(8,128)}, f32[992,256]{1,0:T(8,128)}, f32[96,256]{1,0:T(8,128)}, f32[96,256]{1,0:T(8,128)}, /*index=5*/bf16[1024,256]{1,0:T(8,128)(2,1)}) custom-call(f32[256,256]{1,0:T(8,128)} %get-tuple-element.87.refs_0_, f32[256,256]{1,0:T(8,128)} %copy-done.6, f32[256,256]{1,0:T(8,128)} %copy-done.7, ...), custom_call_target="tpu_custom_call" | custom-call | tf_op jit(solution)/shard_map/block_trees/pallas_call | solution.py:28
  75.8 0.6 copy-done.5
  76.5 12.4 %states_and_sums.1 = (f32[256,256]{1,0:T(8,128)}, f32[8,48,256]{2,1,0:T(8,128)}) custom-call(s32[1,1]{1,0:T(1,128)} %bitcast.refs_0_, bf16[256,256]{1,0:T(8,128)(2,1)} %constant.66.clone.refs_1_, f32[32,2,256]{2,1,0:T(2,128)} %copy-done.5, f32[1024,256]{1,0:T(8,128)} %get-tuple-element.60.refs_3_, f32[992,256]{1,0:T(8,128)} %get-tuple-element.61.refs_4_, ...), custom_call_target="tpu_custom_call" | custom-call | tf_op jit(solution)/shard_map/states_and_sums/pallas_call | solution.py:28
  88.8 20.1 %all_to_all.15.refs_0_ = f32[8,48,256]{2,1,0:T(8,128)} all-to-all(f32[8,48,256]{2,1,0:T(8,128)} %get-tuple-element.78), channel_id=1, replica_groups=mesh['y'=4,'z'=8,'x'=4,'core'=2] {'z'}, dimensions={0} | all-to-all | bytes 786432 | tf_op jit(solution)/shard_map/all_to_all | solution.py:459
  108.9 1.8 %add_pieces.1 = (f32[8,40,256]{2,1,0:T(8,128)}, f32[8,256]{1,0:T(8,128)}) custom-call(f32[8,48,256]{2,1,0:T(8,128)} %all_to_all.15.refs_0_), custom_call_target="tpu_custom_call" | custom-call | tf_op jit(solution)/shard_map/add_pieces/pallas_call | solution.py:28
  110.7 14.6 %all_to_all.16.refs_1_ = f32[8,40,256]{2,1,0:T(8,128)S(1)} all-to-all(f32[8,40,256]{2,1,0:T(8,128)} %get-tuple-element.79), channel_id=1, replica_groups=mesh['y'=4,'z'=8,'x'=4,'core'=2] {'z'}, dimensions={0} | all-to-all | bytes 655360 | tf_op jit(solution)/shard_map/all_to_all | solution.py:465
  125.3 0.5 collective-permute-start.11
  125.8 2.4 %collective-permute-start.12 = (f32[8,40,256]{2,1,0:T(8,128)S(1)}, f32[8,40,256]{2,1,0:T(8,128)S(1)}, u32[]{:S(2)}, u32[]{:S(2)}) collective-permute-start(f32[8,40,256]{2,1,0:T(8,128)S(1)} %all_to_all.16.refs_1_), channel_id=1, source_target_pairs={{0,128},{64,192},{128,0},{192,64},{1,129},{65,193},{129,1},{193,65... | collective-permute-start | bytes 983048 | tf_op jit(solution)/shard_map/ppermute | solution.py:349
  128.2 3.2 %collective-permute-start.14 = (f32[8,256]{1,0:T(8,128)S(1)}, f32[8,256]{1,0:T(8,128)S(1)}, u32[]{:S(2)}, u32[]{:S(2)}) collective-permute-start(f32[8,256]{1,0:T(8,128)S(1)} %copy-done.14), channel_id=1, source_target_pairs={{0,64},{64,128},{128,192},{192,0},{1,65},{65,129},{129,193},{193,1... | collective-permute-start | bytes 24584 | tf_op jit(solution)/shard_map/ppermute | solution.py:349
  131.5 6.2 %collective-permute-done.14.refs_6_ = f32[8,256]{1,0:T(8,128)S(1)} collective-permute-done((f32[8,256]{1,0:T(8,128)S(1)}, f32[8,256]{1,0:T(8,128)S(1)}, u32[]{:S(2)}, u32[]{:S(2)}) %collective-permute-start.14) | collective-permute-done | bytes 8224 | tf_op jit(solution)/shard_map/ppermute | solution.py:349
  137.7 1.8 %collective-permute-done.15.refs_7_ = f32[8,256]{1,0:T(8,128)S(1)} collective-permute-done((f32[8,256]{1,0:T(8,128)S(1)}, f32[8,256]{1,0:T(8,128)S(1)}, u32[]{:S(2)}, u32[]{:S(2)}) %collective-permute-start.15) | collective-permute-done | bytes 8224 | tf_op jit(solution)/shard_map/ppermute | solution.py:349
  139.5 3.1 %collective-permute-done.16.refs_8_ = f32[8,256]{1,0:T(8,128)S(1)} collective-permute-done((f32[8,256]{1,0:T(8,128)S(1)}, f32[8,256]{1,0:T(8,128)S(1)}, u32[]{:S(2)}, u32[]{:S(2)}) %collective-permute-start.16) | collective-permute-done | bytes 8224 | tf_op jit(solution)/shard_map/ppermute | solution.py:349
  142.6 0.5 copy-done.17
  143.6 2.7 %finish.1 = (f32[1024,256]{1,0:T(8,128)}, f32[256,256]{1,0:T(8,128)}, f32[1,1024]{1,0:T(1,128)}) custom-call(s32[1,1]{1,0:T(1,128)} %bitcast.11.refs_0_, f32[8,40,256]{2,1,0:T(8,128)} %copy-done, f32[8,40,256]{2,1,0:T(8,128)} %copy-done.2, f32[8,40,256]{2,1,0:T(8,128)} %copy-done.3, f32[8,40,256]{2,1,0:T(8,128)} %copy-done.4, ...), custom_call_target="tpu_custom_call" | custom-call | tf_op jit(solution)/shard_map/finish/pallas_call | solution.py:28
  (56 shorter events, 1.4 us)
Async XLA Ops:
  3.1 3.6 %collective-permute-start = (f32[128,256]{1,0:T(8,128)}, f32[128,256]{1,0:T(8,128)S(1)}, u32[]{:S(2)}, u32[]{:S(2)}) collective-permute-start(f32[128,256]{1,0:T(8,128)} %get-tuple-element.45), channel_id=1, source_target_pairs={{0,1},{1,0},{2,3},{3,2},{4,5},{5,4},{6,7},{7,6},{8,9},{9,8},{10,11... | collective-permute-start | bytes 393224 | tf_op jit(solution)/shard_map/ppermute | solution.py:349
  5.5 1.3 copy-start.13
  6.8 6.3 %collective-permute-start.3 = (f32[128,256]{1,0:T(8,128)S(1)}, f32[128,256]{1,0:T(8,128)S(1)}, u32[]{:S(2)}, u32[]{:S(2)}) collective-permute-start(f32[128,256]{1,0:T(8,128)S(1)} %add.54), channel_id=1, source_target_pairs={{0,6},{2,0},{4,2},{6,4},{1,7},{3,1},{5,3},{7,5},{8,14},{10,8},{12,... | collective-permute-start | bytes 393224 | tf_op jit(solution)/shard_map/ppermute | solution.py:349
  9.7 9.6 %collective-permute-start.2 = (f32[128,256]{1,0:T(8,128)S(1)}, f32[128,256]{1,0:T(8,128)S(1)}, u32[]{:S(2)}, u32[]{:S(2)}) collective-permute-start(f32[128,256]{1,0:T(8,128)S(1)} %add.54), channel_id=1, source_target_pairs={{0,2},{2,4},{4,6},{6,0},{1,3},{3,5},{5,7},{7,1},{8,10},{10,12},{12... | collective-permute-start | bytes 393224 | tf_op jit(solution)/shard_map/ppermute | solution.py:349
  9.7 9.6 %collective-permute-start.1 = (f32[128,256]{1,0:T(8,128)S(1)}, f32[128,256]{1,0:T(8,128)S(1)}, u32[]{:S(2)}, u32[]{:S(2)}) collective-permute-start(f32[128,256]{1,0:T(8,128)S(1)} %add.54), channel_id=1, source_target_pairs={{0,4},{2,6},{4,0},{6,2},{1,5},{3,7},{5,1},{7,3},{8,12},{10,14},{12... | collective-permute-start | bytes 393224 | tf_op jit(solution)/shard_map/ppermute | solution.py:349
  12.8 31.1 %collective-permute-start.5 = (f32[256,256]{1,0:T(8,128)S(1)}, f32[256,256]{1,0:T(8,128)S(1)}, u32[]{:S(2)}, u32[]{:S(2)}) collective-permute-start(f32[256,256]{1,0:T(8,128)S(1)} %get-tuple-element.86), channel_id=1, source_target_pairs={{0,64},{64,128},{128,192},{192,0},{1,65},{65,129},{129,193},{193,1... | collective-permute-start | bytes 786440 | tf_op jit(solution)/shard_map/ppermute | solution.py:349
  19.4 12.6 %copy-start.1 = (f32[128,256]{1,0:T(8,128)}, f32[128,256]{1,0:T(8,128)S(1)}, u32[]{:S(2)}) copy-start(f32[128,256]{1,0:T(8,128)S(1)} %add_add_fusion.refs_1_) | copy-start | bytes 393220
  19.4 12.6 %collective-permute-start.4 = (f32[128,256]{1,0:T(8,128)S(1)}, f32[128,256]{1,0:T(8,128)S(1)}, u32[]{:S(2)}, u32[]{:S(2)}) collective-permute-start(f32[128,256]{1,0:T(8,128)S(1)} %add_add_fusion.refs_1_), channel_id=1, source_target_pairs={{0,1},{1,0},{2,3},{3,2},{4,5},{5,4},{6,7},{7,6},{8,9},{9,8},{10,11... | collective-permute-start | bytes 393224 | tf_op jit(solution)/shard_map/ppermute | solution.py:349
  19.5 44.4 %collective-permute-start.6 = (f32[256,256]{1,0:T(8,128)S(1)}, f32[256,256]{1,0:T(8,128)S(1)}, u32[]{:S(2)}, u32[]{:S(2)}) collective-permute-start(f32[256,256]{1,0:T(8,128)S(1)} %get-tuple-element.85), channel_id=1, source_target_pairs={{0,128},{64,192},{128,0},{192,64},{1,129},{65,193},{129,1},{193,65... | collective-permute-start | bytes 786440 | tf_op jit(solution)/shard_map/ppermute | solution.py:349
  20.8 43.0 %collective-permute-start.7 = (f32[256,256]{1,0:T(8,128)S(1)}, f32[256,256]{1,0:T(8,128)S(1)}, u32[]{:S(2)}, u32[]{:S(2)}) collective-permute-start(f32[256,256]{1,0:T(8,128)S(1)} %get-tuple-element.84), channel_id=1, source_target_pairs={{0,192},{64,0},{128,64},{192,128},{1,193},{65,1},{129,65},{193,129... | collective-permute-start | bytes 786440 | tf_op jit(solution)/shard_map/ppermute | solution.py:349
  39.6 24.3 %collective-permute-start.8 = (f32[256,256]{1,0:T(8,128)}, f32[256,256]{1,0:T(8,128)S(1)}, u32[]{:S(2)}, u32[]{:S(2)}) collective-permute-start(f32[256,256]{1,0:T(8,128)} %get-tuple-element.59.refs_4_), channel_id=1, source_target_pairs={{0,64},{64,128},{128,192},{192,0},{1,65},{65,129},{129,193},{193,1... | collective-permute-start | bytes 786440 | tf_op jit(solution)/shard_map/ppermute | solution.py:349
  42.8 21.1 %collective-permute-start.9 = (f32[256,256]{1,0:T(8,128)}, f32[256,256]{1,0:T(8,128)S(1)}, u32[]{:S(2)}, u32[]{:S(2)}) collective-permute-start(f32[256,256]{1,0:T(8,128)} %get-tuple-element.59.refs_4_), channel_id=1, source_target_pairs={{0,128},{64,192},{128,0},{192,64},{1,129},{65,193},{129,1},{193,65... | collective-permute-start | bytes 786440 | tf_op jit(solution)/shard_map/ppermute | solution.py:349
  43.9 18.4 %copy-start.6 = (f32[256,256]{1,0:T(8,128)}, f32[256,256]{1,0:T(8,128)S(1)}, u32[]{:S(2)}) copy-start(f32[256,256]{1,0:T(8,128)S(1)} %collective-permute-done.5.refs_1_) | copy-start | bytes 786436
  43.9 20.0 %collective-permute-start.10 = (f32[256,256]{1,0:T(8,128)}, f32[256,256]{1,0:T(8,128)S(1)}, u32[]{:S(2)}, u32[]{:S(2)}) collective-permute-start(f32[256,256]{1,0:T(8,128)} %get-tuple-element.59.refs_4_), channel_id=1, source_target_pairs={{0,192},{64,0},{128,64},{192,128},{1,193},{65,1},{129,65},{193,129... | collective-permute-start | bytes 786440 | tf_op jit(solution)/shard_map/ppermute | solution.py:349
  44.6 31.2 %all-to-all-start = ((f32[32,2,256]{2,1,0:T(2,128)}), f32[32,2,256]{2,1,0:T(2,128)S(1)}, u32[]{:S(2)}, u32[]{:S(2)}) async-start(f32[32,2,256]{2,1,0:T(2,128)} %get-tuple-element.54), calls=%async_computation | async-start | bytes 131072 | tf_op jit(solution)/shard_map/all_to_all | solution.py:418
  63.8 0.8 copy-start.8
  63.9 0.8 copy-start.9
  63.9 0.9 copy-start.10
  63.9 1.0 copy-start.11
  110.7 17.5 %copy-start.14 = (f32[8,256]{1,0:T(8,128)S(1)}, f32[8,256]{1,0:T(8,128)}, u32[]{:S(2)}) copy-start(f32[8,256]{1,0:T(8,128)} %get-tuple-element.80.refs_5_) | copy-start | bytes 24580
  125.3 17.3 %copy-start = (f32[8,40,256]{2,1,0:T(8,128)}, f32[8,40,256]{2,1,0:T(8,128)S(1)}, u32[]{:S(2)}) copy-start(f32[8,40,256]{2,1,0:T(8,128)S(1)} %all_to_all.16.refs_1_) | copy-start | bytes 983044
  125.3 17.2 %collective-permute-start.11 = (f32[8,40,256]{2,1,0:T(8,128)S(1)}, f32[8,40,256]{2,1,0:T(8,128)S(1)}, u32[]{:S(2)}, u32[]{:S(2)}) collective-permute-start(f32[8,40,256]{2,1,0:T(8,128)S(1)} %all_to_all.16.refs_1_), channel_id=1, source_target_pairs={{0,64},{64,128},{128,192},{192,0},{1,65},{65,129},{129,193},{193,1... | collective-permute-start | bytes 983048 | tf_op jit(solution)/shard_map/ppermute | solution.py:349
  125.8 16.7 %collective-permute-start.12 = (f32[8,40,256]{2,1,0:T(8,128)S(1)}, f32[8,40,256]{2,1,0:T(8,128)S(1)}, u32[]{:S(2)}, u32[]{:S(2)}) collective-permute-start(f32[8,40,256]{2,1,0:T(8,128)S(1)} %all_to_all.16.refs_1_), channel_id=1, source_target_pairs={{0,128},{64,192},{128,0},{192,64},{1,129},{65,193},{129,1},{193,65... | collective-permute-start | bytes 983048 | tf_op jit(solution)/shard_map/ppermute | solution.py:349
  128.2 14.4 %collective-permute-start.13 = (f32[8,40,256]{2,1,0:T(8,128)S(1)}, f32[8,40,256]{2,1,0:T(8,128)S(1)}, u32[]{:S(2)}, u32[]{:S(2)}) collective-permute-start(f32[8,40,256]{2,1,0:T(8,128)S(1)} %all_to_all.16.refs_1_), channel_id=1, source_target_pairs={{0,192},{64,0},{128,64},{192,128},{1,193},{65,1},{129,65},{193,129... | collective-permute-start | bytes 983048 | tf_op jit(solution)/shard_map/ppermute | solution.py:349
  128.2 9.5 %collective-permute-start.14 = (f32[8,256]{1,0:T(8,128)S(1)}, f32[8,256]{1,0:T(8,128)S(1)}, u32[]{:S(2)}, u32[]{:S(2)}) collective-permute-start(f32[8,256]{1,0:T(8,128)S(1)} %copy-done.14), channel_id=1, source_target_pairs={{0,64},{64,128},{128,192},{192,0},{1,65},{65,129},{129,193},{193,1... | collective-permute-start | bytes 24584 | tf_op jit(solution)/shard_map/ppermute | solution.py:349
  131.4 8.0 %collective-permute-start.15 = (f32[8,256]{1,0:T(8,128)S(1)}, f32[8,256]{1,0:T(8,128)S(1)}, u32[]{:S(2)}, u32[]{:S(2)}) collective-permute-start(f32[8,256]{1,0:T(8,128)S(1)} %copy-done.14), channel_id=1, source_target_pairs={{0,128},{64,192},{128,0},{192,64},{1,129},{65,193},{129,1},{193,65... | collective-permute-start | bytes 24584 | tf_op jit(solution)/shard_map/ppermute | solution.py:349
  137.7 4.9 %copy-start.15 = (f32[8,256]{1,0:T(8,128)}, f32[8,256]{1,0:T(8,128)S(1)}, u32[]{:S(2)}) copy-start(f32[8,256]{1,0:T(8,128)S(1)} %collective-permute-done.14.refs_6_) | copy-start | bytes 24580
  137.7 4.9 %collective-permute-start.16 = (f32[8,256]{1,0:T(8,128)S(1)}, f32[8,256]{1,0:T(8,128)S(1)}, u32[]{:S(2)}, u32[]{:S(2)}) collective-permute-start(f32[8,256]{1,0:T(8,128)S(1)} %copy-done.14), channel_id=1, source_target_pairs={{0,192},{64,0},{128,64},{192,128},{1,193},{65,1},{129,65},{193,129... | collective-permute-start | bytes 24584 | tf_op jit(solution)/shard_map/ppermute | solution.py:349
  139.5 3.2 %copy-start.16 = (f32[8,256]{1,0:T(8,128)}, f32[8,256]{1,0:T(8,128)S(1)}, u32[]{:S(2)}) copy-start(f32[8,256]{1,0:T(8,128)S(1)} %collective-permute-done.15.refs_7_) | copy-start | bytes 24580
  142.6 0.7 copy-start.2
  142.6 0.9 copy-start.3
  142.6 1.0 copy-start.4
  (4 other events, 2.6 us)

commit v2 on v1

--- a/solution.py
+++ b/solution.py
@@ -16,19 +16,33 @@
 KERNELS = True
 
 
-def call(body, outs, *args):
+def call(body, outs, *args, limit=16, scalars=(), hbm=()):
     if not KERNELS:
-        return body(*args)
+        return body(*[arg[0, 0] if i in scalars else arg for i, arg in enumerate(args)])
 
     def kernel(*refs):
-        values = body(*[ref[...] for ref in refs[: len(args)]])
+        values = body(
+            *[ref[0, 0] if i in scalars else ref[...] for i, ref in enumerate(refs[: len(args)])]
+        )
         for ref, value in zip(refs[len(args) :], values):
             ref[...] = value
 
+    args = [
+        arg if i in scalars else pltpu.with_memory_space_constraint(arg, pltpu.VMEM)
+        for i, arg in enumerate(args)
+    ]
     return pl.pallas_call(
         kernel,
-        out_shape=[jax.ShapeDtypeStruct(shape, dtype) for shape, dtype in outs],
-        compiler_params=pltpu.CompilerParams(vmem_limit_bytes=56 * 2**20),
+        out_shape=[
+            jax.ShapeDtypeStruct(shape, dtype) if i in hbm else pltpu.VMEM(shape, dtype)
+            for i, (shape, dtype) in enumerate(outs)
+        ],
+        in_specs=[
+            pl.BlockSpec(memory_space=pltpu.SMEM if i in scalars else pltpu.VMEM)
+            for i in range(len(args))
+        ],
+        out_specs=[pl.BlockSpec(memory_space=pltpu.VMEM)] * len(outs),
+        compiler_params=pltpu.CompilerParams(vmem_limit_bytes=limit * 2**20),
         name=body.__name__,
     )(*args)
 
@@ -37,6 +51,12 @@
     if KERNELS:
         return pltpu.roll(rows, by % rows.shape[0], 0)
     return jnp.roll(rows, by, 0)
+
+
+def roll_lanes(rows, by):
+    if KERNELS:
+        return pltpu.roll(rows, by, 1)
+    return jnp.roll(rows, by, 1)
 
 
 def row_index(rows):
@@ -108,16 +128,27 @@
     weighted = (emission.astype(F32) * scale).astype(BF16)
     information = dot(rows, weighted)
     half = rows.shape[0] // 2
-    first = jnp.broadcast_to(core, (half, information.shape[1])) == 0
+    first = core == 0
     mine = jnp.where(first, information[:half], information[half:])
     other = jnp.where(first, information[half:], information[:half])
     return mine, other
 
 
-def channel_slices(order, observations):
+def chosen(number, values):
+    out = values[0]
+    for i in range(1, len(values)):
+        out = jnp.where(number == i, values[i], out)
+    return out
+
+
+def channel_slices(y, order, observations, emission):
     rows = dot(order, observations)
     width = rows.shape[1] // N_Y
-    return tuple(rows[:, i * width : (i + 1) * width] for i in range(N_Y))
+    parts = [rows[:, i * width : (i + 1) * width] for i in range(N_Y)]
+    emission = emission.astype(F32)
+    emission = chosen(y, [emission[i * width : (i + 1) * width] for i in range(N_Y)])
+    turned = [chosen(y, [parts[(i + by) % N_Y] for i in range(N_Y)]) for by in range(N_Y)]
+    return (*turned, emission.astype(BF16))
 
 
 def up_sweep(lead, a_cut, b_cut, m_cut, information):
@@ -151,7 +182,7 @@
 
 
 def block_ends(core, total, theirs, lead_h, lead_l, a_h, a_l, b_h, b_l, m_h, m_l):
-    first = jnp.broadcast_to(core, total.shape) == 0
+    first = core == 0
     information = jnp.concatenate(
         [jnp.where(first, total, theirs), jnp.where(first, theirs, total)], axis=0
     )
@@ -244,7 +275,7 @@
 
     place = lax.broadcasted_iota(jnp.int32, (N_Y * SUB, BLOCKS), 0)
     source = lax.broadcasted_iota(jnp.int32, (N_Y * SUB, BLOCKS), 1)
-    wanted = jnp.broadcast_to(block, place.shape) - N_Z * (place // SUB)
+    wanted = block - N_Z * (place // SUB)
     pick = (source == jnp.where(wanted < 0, wanted + BLOCKS, wanted)).astype(BF16)
 
     def picked(rows):
@@ -298,18 +329,21 @@
         out = out + dot(natural, high)
 
     channels = cross.shape[0]
-    share = moment.shape[0] // N_Y
-    y = jnp.broadcast_to(block, (share, width)) // N_Z
-    mine = moment[:share]
-    for i in range(1, N_Y):
-        mine = jnp.where(y == i, moment[i * share : (i + 1) * share], mine)
+    share, line = width // N_Y, channels // N_Z
+    y = block // N_Z
+    mine = chosen(y, [moment[i * share : (i + 1) * share] for i in range(N_Y)])
+    free = share * jnp.where(y == N_Y - 1, 0, y + 1)
+    lane = lax.broadcasted_iota(jnp.int32, (8, width), 1)
+    row = lax.broadcasted_iota(jnp.int32, (8, width), 0)
+    is_free = (lane >= free) & (lane < free + share)
+    is_error = (lane >= free) & (lane < free + line) & (row == 0)
+    chunks = []
+    for z in range(N_Z):
+        turned = roll_lanes(error, free + (width - line * z))
+        tile = jnp.where(is_free, 0.0, mine[8 * z : 8 * z + 8])
+        chunks.append(jnp.where(is_error, turned, tile))
     payload = jnp.concatenate(
-        [
-            cross.reshape(N_Z, channels // N_Z, width),
-            mine.reshape(N_Z, share // N_Z, width),
-            jnp.broadcast_to(error[None], (N_Z,) + error.shape),
-        ],
-        axis=1,
+        [cross.reshape(N_Z, line, width), jnp.stack(chunks)], axis=1
     )
     return out, payload
 
@@ -318,31 +352,30 @@
     total = pieces[0]
     for i in range(1, N_Z):
         total = total + pieces[i]
-    kept = total.shape[0] - 8
-    return jnp.broadcast_to(total[None, :kept], (N_Z, kept, total.shape[1])), total[kept:]
-
-
-def assemble(bins, channel_rows, place, sums, errors):
+    return (jnp.broadcast_to(total[None], (N_Z,) + total.shape),)
+
+
+def assemble(bins, place, *sums):
     width = sums[0].shape[2]
-    cross, moment, error = [], [], []
-    for i in range(N_Y):
-        want = jnp.broadcast_to(place, sums[0].shape) - i
-        want = jnp.where(want < 0, want + N_Y, want)
-        whole = sums[0]
-        for by in range(1, N_Y):
-            whole = jnp.where(want == by, sums[by], whole)
-        cross.append(whole[:, :channel_rows].reshape(-1, width) * (1.0 / math.sqrt(bins)))
-        moment.append(whole[:, channel_rows:].reshape(-1, width) * (1.0 / bins))
-        want = want[0, :8]
-        line = errors[0]
-        for by in range(1, N_Y):
-            line = jnp.where(want == by, errors[by], line)
-        error.append(line[:1] * (1.0 / bins))
-    return (
-        jnp.concatenate(cross, axis=0),
-        jnp.concatenate(moment, axis=0),
-        jnp.concatenate(error, axis=1),
-    )
+    share = width // N_Y
+    line = sums[0].shape[1] - 8
+    lane = lax.broadcasted_iota(jnp.int32, (8, width), 1)
+    cross, moment, errors = [], [], []
+    for y in range(N_Y):
+        whole = chosen(place, [sums[(i - y) % N_Y] for i in range(N_Y)])
+        cross.append(whole[:, :line].reshape(-1, width) * (1.0 / math.sqrt(bins)))
+        moment.append(whole[:, line:].reshape(-1, width))
+        error = jnp.zeros((8, width), F32)
+        for z in range(N_Z):
+            turned = roll_lanes(whole[z, line:], (line * z - share * ((y + 1) % N_Y)) % width)
+            error = jnp.where((lane >= line * z) & (lane < line * z + line), turned, error)
+        errors.append(error[:1] * (1.0 / bins))
+    moment = jnp.concatenate(moment, axis=0)
+    row = lax.broadcasted_iota(jnp.int32, moment.shape, 0) // share
+    column = lax.broadcasted_iota(jnp.int32, moment.shape, 1) // share
+    free = column == jnp.where(row == N_Y - 1, 0, row + 1)
+    moment = jnp.where(free, moment.T, moment) * (1.0 / bins)
+    return jnp.concatenate(cross, axis=0), moment, jnp.concatenate(errors, axis=1)
 
 
 def shift(value, axis, count, by):
@@ -378,17 +411,23 @@
         observations,
         emission,
         noise_precision.reshape(1, channels),
+        scalars=(0,),
     )
     mine = mine + shift(other, "core", N_CORE, 1)
+    mine, later = lax.optimization_barrier((mine, observations))
     moved = [shift(mine, "x", N_X, by) for by in (2, 1, 3)]
 
-    slices = call(channel_slices, [((bins, channels // N_Y), F32)] * N_Y, order, observations)
-    slices = jnp.stack(slices)
-    piece = lambda by: lax.dynamic_index_in_dim(slices, (y + by) % N_Y, 0, False)
-    observed = [piece(0)] + [shift(piece(by), "y", N_Y, by) for by in (1, 2, 3)]
-    emission_part = lax.dynamic_slice_in_dim(
-        emission, y * (channels // N_Y), channels // N_Y, 0
-    )
+    part = channels // N_Y
+    *slices, emission_part = call(
+        channel_slices,
+        [((bins, part), F32)] * N_Y + [((part, width), BF16)],
+        one(y),
+        order,
+        later,
+        emission,
+        scalars=(0,),
+    )
+    observed = slices[:1] + [shift(slices[by], "y", N_Y, by) for by in (1, 2, 3)]
 
     square = (width, width)
     stack = lambda n: [((n,) + square, BF16)] * 2
@@ -414,6 +453,7 @@
         *a_cut,
         *b_cut,
         *m_cut,
+        scalars=(0,),
     )
     gathered = lax.all_to_all(ends, ("y", "z"), 0, 0)
     informations = [information] + [shift(information, "y", N_Y, by) for by in (1, 2, 3)]
@@ -436,10 +476,10 @@
         *b_cut,
         *m_cut,
     )
-    channel_rows, moment_rows = channels // (N_Y * N_Z), width // (N_Y * N_Z)
+    rows = channels // (N_Y * N_Z) + 8
     smoothed, payload = call(
         states_and_sums,
-        [((bins, width), F32), ((N_Z, channel_rows + moment_rows + 8, width), F32)],
+        [((bins, width), F32), ((N_Z, rows, width), F32)],
         one(lax.axis_index(("y", "z"))),
         natural,
         gathered,
@@ -455,27 +495,26 @@
         *b_cut,
         *n_cut,
         *big,
+        scalars=(0,),
     )
     payload = lax.all_to_all(payload, "z", 0, 0)
-    spread, error = call(
-        add_pieces,
-        [((N_Z, channel_rows + moment_rows, width), F32), ((8, width), F32)],
-        payload,
-    )
+    (spread,) = call(add_pieces, [((N_Z, rows, width), F32)], payload)
     whole = lax.all_to_all(spread, "z", 0, 0)
-    errors = [error] + [shift(error, "y", N_Y, by) for by in (1, 2, 3)]
-    sums = [whole] + [shift(whole, "y", N_Y, by) for by in (2, 1, 3)]
-    sums = [sums[0], sums[2], sums[1], sums[3]]
-
-    def finish(place, s0, s1, s2, s3, e0, e1, e2, e3):
-        return assemble(bins * BLOCKS, channel_rows, place, [s0, s1, s2, s3], [e0, e1, e2, e3])
+    far, near, back = (shift(whole, "y", N_Y, by) for by in (2, 1, 3))
+
+    def finish(*args):
+        return assemble(bins * BLOCKS, *args)
 
     cross, moment, error = call(
         finish,
         [((channels, width), F32), (square, F32), ((1, channels), F32)],
         one(y),
-        *sums,
-        *errors,
+        whole,
+        near,
+        far,
+        back,
+        scalars=(0,),
+        hbm=(0, 1, 2),
     )
     return smoothed, cross, error.reshape(channels), moment
 

time: 147 us -> 157 us (1.068); the launches traced: 146 us -> 154 us
  local copies, waits for them, and re-layouts: 5.58 us -> 44.8 us
  Pallas kernels: 55.9 us -> 31 us
  blocking collectives: 34.7 us -> 32 us
    unnamed x36 -> x127, local copies, waits for them, and re-layouts: 3.24 us -> 44.8 us
    pallas_call x9, Pallas kernels: 55.9 us -> 31 us  [call(): pl.pallas_call(kernel, out_shape=[jax.ShapeDtypeStruct(shape, dtype) if i...]
    all_to_all x1, blocking collectives: 20.1 us -> 18.4 us  [local(): payload = lax.all_to_all(payload, 'z', 0, 0)]
    ppermute x17 -> x14, waiting for transfers between devices: 17.4 us -> 16.6 us  [shift(): lax.ppermute(value, axis, [(i, (i + by) % count) for i in range(count)])]
    ppermute x17 -> x14, starting transfers between devices: 18 us -> 17.5 us  [shift(): lax.ppermute(value, axis, [(i, (i + by) % count) for i in range(count)])]
  transfers between devices with their start and end apart: 18 -> 15, of which waited for: 5 -> 4; matrix products, arithmetic and copies ran while one was open for 3% -> 0% of each run, Pallas kernels for 25% -> 14%
where the time goes in v2:
time: 157 us; the launch traced here: 154 us
  local copies, waits for them, and re-layouts  44.8 us (29%)
  blocking collectives  32 us (20%)
  Pallas kernels  31 us (20%)
  starting transfers between devices  29 us (18%)
  waiting for transfers between devices  16.6 us (11%)
    unnamed x127, local copies, waits for them, and re-layouts  44.8 us
    pallas_call x9, Pallas kernels, call(): pl.pallas_call(kernel, out_shape=[jax.ShapeDtypeStruct(shape, dtype) if i...  31 us
    all_to_all x1, blocking collectives, local(): payload = lax.all_to_all(payload, 'z', 0, 0)  18.4 us
    ppermute x14, starting transfers between devices, shift(): lax.ppermute(value, axis, [(i, (i + by) % count) for i in range(count)])  17.5 us
    ppermute x14, waiting for transfers between devices, shift(): lax.ppermute(value, axis, [(i, (i + by) % count) for i in range(count)])  16.6 us
    all_to_all x1, blocking collectives, local(): whole = lax.all_to_all(spread, 'z', 0, 0)  13.6 us
    all_to_all x1, starting transfers between devices, local(): gathered = lax.all_to_all(ends, ('y', 'z'), 0, 0)  11.6 us
  transfers between devices with their start and end apart: 15, of which 4 were waited for; matrix products, arithmetic and copies ran while one was open for 0% of the time, Pallas kernels for 14%

profile of v2, /device:TPU:24, one launch (start us, length us, event | category | flops | bytes accessed | tf_op | source)
XLA Modules:
  0.0 154.4 jit_solution(15352313986179848251)
XLA Ops:
  5.0 1.3 collective-permute-done
  6.3 2.8 %collective-permute-start.3 = (f32[128,256]{1,0:T(8,128)S(1)}, f32[128,256]{1,0:T(8,128)S(1)}, u32[]{:S(2)}, u32[]{:S(2)}) collective-permute-start(f32[128,256]{1,0:T(8,128)S(1)} %add.16), channel_id=1, source_target_pairs={{0,6},{2,0},{4,2},{6,4},{1,7},{3,1},{5,3},{7,5},{8,14},{10,8},{12,... | collective-permute-start | bytes 393224 | tf_op jit(solution)/shard_map/ppermute | solution.py:382
  9.2 2.3 %collective-permute-start.1 = (f32[128,256]{1,0:T(8,128)S(1)}, f32[128,256]{1,0:T(8,128)S(1)}, u32[]{:S(2)}, u32[]{:S(2)}) collective-permute-start(f32[128,256]{1,0:T(8,128)S(1)} %add.16), channel_id=1, source_target_pairs={{0,4},{2,6},{4,0},{6,2},{1,5},{3,7},{5,1},{7,3},{8,12},{10,14},{12... | collective-permute-start | bytes 393224 | tf_op jit(solution)/shard_map/ppermute | solution.py:382
  11.5 1.1 channel_slices.1
  12.9 5.6 %collective-permute-done.2 = f32[128,256]{1,0:T(8,128)S(1)} collective-permute-done((f32[128,256]{1,0:T(8,128)S(1)}, f32[128,256]{1,0:T(8,128)S(1)}, u32[]{:S(2)}, u32[]{:S(2)}) %collective-permute-start.2) | collective-permute-done | bytes 131104 | tf_op jit(solution)/shard_map/ppermute | solution.py:382
  18.8 7.4 %small_powers.1 = (bf16[5,256,256]{2,1,0:T(8,128)(2,1)S(1)}, bf16[5,256,256]{2,1,0:T(8,128)(2,1)S(1)}, bf16[8,256,256]{2,1,0:T(8,128)(2,1)S(1)}, bf16[8,256,256]...) custom-call(f32[256,256]{1,0:T(8,128)S(1)} %copy-done.47, ...), custom_call_target="tpu_custom_call" | custom-call | tf_op jit(solution)/shard_map/small_powers/pallas_call | solution.py:34
  27.2 1.3 collective-permute-start.6
  28.6 3.6 %block_ends.1 = (f32[256,256]{1,0:T(8,128)}, f32[32,2,256]{2,1,0:T(2,128)}) custom-call(s32[1,1]{1,0:T(1,128)} %bitcast.1.refs_0_, f32[128,256]{1,0:T(8,128)S(1)} %add_add_fusion.refs_1_, f32[128,256]{1,0:T(8,128)S(1)} %collective-permute-done.4.refs_2_, bf16[5,256,256]{2,1,0:T(8,128)(2,1)S(1)} %get-tuple-element.48.refs_3_.refs_8_.refs_10_, ...), custom_call_target="tpu_custom_call" | custom-call | tf_op jit(solution)/shard_map/block_ends/pallas_call | solution.py:34
  32.2 2.3 %collective-permute-start.10 = (f32[256,256]{1,0:T(8,128)}, f32[256,256]{1,0:T(8,128)}, u32[]{:S(2)}, u32[]{:S(2)}) collective-permute-start(f32[256,256]{1,0:T(8,128)} %get-tuple-element.62.refs_4_), channel_id=1, source_target_pairs={{0,192},{64,0},{128,64},{192,128},{1,193},{65,1},{129,65},{193,129... | collective-permute-start | bytes 786440 | tf_op jit(solution)/shard_map/ppermute | solution.py:382
  34.5 2.5 %collective-permute-start.9 = (f32[256,256]{1,0:T(8,128)}, f32[256,256]{1,0:T(8,128)}, u32[]{:S(2)}, u32[]{:S(2)}) collective-permute-start(f32[256,256]{1,0:T(8,128)} %get-tuple-element.62.refs_4_), channel_id=1, source_target_pairs={{0,128},{64,192},{128,0},{192,64},{1,129},{65,193},{129,1},{193,65... | collective-permute-start | bytes 786440 | tf_op jit(solution)/shard_map/ppermute | solution.py:382
  37.7 1.6 %collective-permute-start.8 = (f32[256,256]{1,0:T(8,128)}, f32[256,256]{1,0:T(8,128)}, u32[]{:S(2)}, u32[]{:S(2)}) collective-permute-start(f32[256,256]{1,0:T(8,128)} %get-tuple-element.62.refs_4_), channel_id=1, source_target_pairs={{0,64},{64,128},{128,192},{192,0},{1,65},{65,129},{129,193},{193,1... | collective-permute-start | bytes 786440 | tf_op jit(solution)/shard_map/ppermute | solution.py:382
  39.2 11.6 %all-to-all-start = ((f32[32,2,256]{2,1,0:T(2,128)}), f32[32,2,256]{2,1,0:T(2,128)S(1)}, u32[]{:S(2)}, u32[]{:S(2)}) async-start(f32[32,2,256]{2,1,0:T(2,128)} %get-tuple-element.56), calls=%async_computation | async-start | bytes 131072 | tf_op jit(solution)/shard_map/all_to_all | solution.py:458
  53.8 2.5 %big_powers.1 = (bf16[5,256,256]{2,1,0:T(8,128)(2,1)S(1)}, bf16[5,256,256]{2,1,0:T(8,128)(2,1)S(1)}, bf16[5,256,256]{2,1,0:T(8,128)(2,1)S(1)}, bf16[5,256,256]{2...) custom-call(f32[256,256]{1,0:T(8,128)S(1)} %copy-done.42, f32[256,256]{1,0:T(8,128)S(1)} %copy-done.44, ...), custom_call_target="tpu_custom_call" | custom-call | tf_op jit(solution)/shard_map/big_powers/pallas_call | solution.py:34
  61.0 1.2 copy-done.1
  62.2 1.1 copy-done.7
  63.3 1.2 copy-done.10
  64.5 1.2 copy-done.12
  66.7 7.8 %block_trees.1 = (f32[1024,256]{1,0:T(8,128)S(1)}, f32[992,256]{1,0:T(8,128)S(1)}, f32[992,256]{1,0:T(8,128)S(1)}, f32[96,256]{1,0:T(8,128)S(1)}, f32[96,256]{1,0:T(8,128)S(1)}, /*index=5*/bf16[1024,256]{1,0:T(8,128)(2,1)S(1)}) custom-call(f32[256,256]{1,0:T(8,128)S(1)} %get-tuple-element.58.refs_0_, f32[256,256]{1,0:T(8,128)S(1)} %copy-done.40, ...), custom_call_target="tpu_custom_call" | custom-call | tf_op jit(solution)/shard_map/block_trees/pallas_call | solution.py:34
  79.6 1.2 copy-done.2
  81.9 1.1 copy-done.8
  83.0 1.2 copy-done.18
  84.3 1.2 copy-done.20
  85.5 1.2 copy-done.22
  86.7 1.2 copy-done.24
  87.9 1.2 copy-done.26
  99.9 6.5 %states_and_sums.1 = (f32[256,256]{1,0:T(8,128)S(1)}, f32[8,40,256]{2,1,0:T(8,128)S(1)}) custom-call(s32[1,1]{1,0:T(1,128)} %bitcast.refs_0_, bf16[256,256]{1,0:T(8,128)(2,1)S(1)} %copy-done.51, f32[32,2,256]{2,1,0:T(2,128)S(1)} %all-to-all-done.refs_2_, f32[1024,256]{1,0:T(8,128)S(1)} %copy-done.22, f32[992,256]{1,0:T(8,128)S(1)} %copy-done.24, ...), custom_call_target="tpu_custom_call" | custom-call | tf_op jit(solution)/shard_map/states_and_sums/pallas_call | solution.py:34
  106.5 18.4 %all_to_all.15.refs_0_ = f32[8,40,256]{2,1,0:T(8,128)S(1)} all-to-all(f32[8,40,256]{2,1,0:T(8,128)S(1)} %get-tuple-element.82), channel_id=1, replica_groups=mesh['y'=4,'z'=8,'x'=4,'core'=2] {'z'}, dimensions={0} | all-to-all | bytes 655360 | tf_op jit(solution)/shard_map/all_to_all | solution.py:500
  124.9 13.6 %all_to_all.16.refs_1_ = f32[8,40,256]{2,1,0:T(8,128)S(1)} all-to-all(f32[8,40,256]{2,1,0:T(8,128)S(1)} %add_pieces.1), channel_id=1, replica_groups=mesh['y'=4,'z'=8,'x'=4,'core'=2] {'z'}, dimensions={0} | all-to-all | bytes 655360 | tf_op jit(solution)/shard_map/all_to_all | solution.py:502
  139.3 1.2 collective-permute-start.12
  140.4 2.1 %collective-permute-start.11 = (f32[8,40,256]{2,1,0:T(8,128)S(1)}, f32[8,40,256]{2,1,0:T(8,128)S(1)}, u32[]{:S(2)}, u32[]{:S(2)}) collective-permute-start(f32[8,40,256]{2,1,0:T(8,128)S(1)} %all_to_all.16.refs_1_), channel_id=1, source_target_pairs={{0,64},{64,128},{128,192},{192,0},{1,65},{65,129},{129,193},{193,1... | collective-permute-start | bytes 983048 | tf_op jit(solution)/shard_map/ppermute | solution.py:382
  143.2 9.0 %collective-permute-done.13.refs_4_ = f32[8,40,256]{2,1,0:T(8,128)S(1)} collective-permute-done((f32[8,40,256]{2,1,0:T(8,128)S(1)}, f32[8,40,256]{2,1,0:T(8,128)S(1)}, u32[]{:S(2)}, u32[]{:S(2)}) %collective-permute-start.13) | collective-permute-done | bytes 327712 | tf_op jit(solution)/shard_map/ppermute | solution.py:382
  152.8 1.5 finish.1
  (138 shorter events, 34.3 us)
Async XLA Ops:
  4.3 7.1 %copy-start.14 = (bf16[256,1024]{1,0:T(8,128)(2,1)S(1)}, bf16[256,1024]{1,0:T(8,128)(2,1)}, u32[]{:S(2)}) copy-start(bf16[256,1024]{1,0:T(8,128)(2,1)} %refs_2_.4) | copy-start | bytes 1572868
  4.3 7.1 %copy-start.16 = (bf16[1024,256]{1,0:T(8,128)(2,1)S(1)}, bf16[1024,256]{1,0:T(8,128)(2,1)}, u32[]{:S(2)}) copy-start(bf16[1024,256]{1,0:T(8,128)(2,1)} %refs_3_.5) | copy-start | bytes 1572868
  4.9 1.4 collective-permute-start
  6.3 5.2 %copy-start.38 = (bf16[256,256]{1,0:T(8,128)(2,1)S(1)}, bf16[256,256]{1,0:T(8,128)(2,1)}, u32[]{:S(2)}) copy-start(bf16[256,256]{1,0:T(8,128)(2,1)} %constant.20.clone.refs_1_) | copy-start | bytes 393220
  6.3 6.6 %collective-permute-start.3 = (f32[128,256]{1,0:T(8,128)S(1)}, f32[128,256]{1,0:T(8,128)S(1)}, u32[]{:S(2)}, u32[]{:S(2)}) collective-permute-start(f32[128,256]{1,0:T(8,128)S(1)} %add.16), channel_id=1, source_target_pairs={{0,6},{2,0},{4,2},{6,4},{1,7},{3,1},{5,3},{7,5},{8,14},{10,8},{12,... | collective-permute-start | bytes 393224 | tf_op jit(solution)/shard_map/ppermute | solution.py:382
  9.2 9.3 %collective-permute-start.2 = (f32[128,256]{1,0:T(8,128)S(1)}, f32[128,256]{1,0:T(8,128)S(1)}, u32[]{:S(2)}, u32[]{:S(2)}) collective-permute-start(f32[128,256]{1,0:T(8,128)S(1)} %add.16), channel_id=1, source_target_pairs={{0,2},{2,4},{4,6},{6,0},{1,3},{3,5},{5,7},{7,1},{8,10},{10,12},{12... | collective-permute-start | bytes 393224 | tf_op jit(solution)/shard_map/ppermute | solution.py:382
  9.2 9.3 %collective-permute-start.1 = (f32[128,256]{1,0:T(8,128)S(1)}, f32[128,256]{1,0:T(8,128)S(1)}, u32[]{:S(2)}, u32[]{:S(2)}) collective-permute-start(f32[128,256]{1,0:T(8,128)S(1)} %add.16), channel_id=1, source_target_pairs={{0,4},{2,6},{4,0},{6,2},{1,5},{3,7},{5,1},{7,3},{8,12},{10,14},{12... | collective-permute-start | bytes 393224 | tf_op jit(solution)/shard_map/ppermute | solution.py:382
  11.5 7.3 %copy-start.49 = (f32[256,256]{1,0:T(8,128)S(1)}, f32[256,256]{1,0:T(8,128)}, u32[]{:S(2)}) copy-start(f32[256,256]{1,0:T(8,128)} %refs_2_.3) | copy-start | bytes 786436
  11.5 7.3 %copy-start.50 = (f32[256,256]{1,0:T(8,128)S(1)}, f32[256,256]{1,0:T(8,128)}, u32[]{:S(2)}) copy-start(f32[256,256]{1,0:T(8,128)} %refs_3_.4) | copy-start | bytes 786436
  12.6 5.9 %copy-start.52 = (bf16[256,256]{1,0:T(8,128)(2,1)}, bf16[256,256]{1,0:T(8,128)(2,1)S(1)}, u32[]{:S(2)}) copy-start(bf16[256,256]{1,0:T(8,128)(2,1)S(1)} %get-tuple-element.69.refs_9_) | copy-start | bytes 393220
  12.6 6.2 %copy-start.47 = (f32[256,256]{1,0:T(8,128)S(1)}, f32[256,256]{1,0:T(8,128)}, u32[]{:S(2)}) copy-start(f32[256,256]{1,0:T(8,128)} %refs_0_.1) | copy-start | bytes 786436
  12.6 6.2 %copy-start.48 = (f32[256,256]{1,0:T(8,128)S(1)}, f32[256,256]{1,0:T(8,128)}, u32[]{:S(2)}) copy-start(f32[256,256]{1,0:T(8,128)} %refs_1_.4) | copy-start | bytes 786436
  12.6 24.4 %collective-permute-start.5 = (f32[256,256]{1,0:T(8,128)S(1)}, f32[256,256]{1,0:T(8,128)S(1)}, u32[]{:S(2)}, u32[]{:S(2)}) collective-permute-start(f32[256,256]{1,0:T(8,128)S(1)} %get-tuple-element.59), channel_id=1, source_target_pairs={{0,64},{64,128},{128,192},{192,0},{1,65},{65,129},{129,193},{193,1... | collective-permute-start | bytes 786440 | tf_op jit(solution)/shard_map/ppermute | solution.py:382
  18.5 10.1 %collective-permute-start.4 = (f32[128,256]{1,0:T(8,128)S(1)}, f32[128,256]{1,0:T(8,128)S(1)}, u32[]{:S(2)}, u32[]{:S(2)}) collective-permute-start(f32[128,256]{1,0:T(8,128)S(1)} %add_add_fusion.refs_1_), channel_id=1, source_target_pairs={{0,1},{1,0},{2,3},{3,2},{4,5},{5,4},{6,7},{7,6},{8,9},{9,8},{10,11... | collective-permute-start | bytes 393224 | tf_op jit(solution)/shard_map/ppermute | solution.py:382
  27.2 5.0 %copy-start.3 = (bf16[5,256,256]{2,1,0:T(8,128)(2,1)}, bf16[5,256,256]{2,1,0:T(8,128)(2,1)S(1)}, u32[]{:S(2)}) copy-start(bf16[5,256,256]{2,1,0:T(8,128)(2,1)S(1)} %get-tuple-element.48.refs_3_.refs_8_.refs_10_) | copy-start | bytes 1966084
  27.2 5.0 %copy-start.6 = (bf16[5,256,256]{2,1,0:T(8,128)(2,1)}, bf16[5,256,256]{2,1,0:T(8,128)(2,1)S(1)}, u32[]{:S(2)}) copy-start(bf16[5,256,256]{2,1,0:T(8,128)(2,1)S(1)} %get-tuple-element.49.refs_4_.refs_9_.refs_11_) | copy-start | bytes 1966084
  27.2 5.0 %copy-start.9 = (bf16[8,256,256]{2,1,0:T(8,128)(2,1)}, bf16[8,256,256]{2,1,0:T(8,128)(2,1)S(1)}, u32[]{:S(2)}) copy-start(bf16[8,256,256]{2,1,0:T(8,128)(2,1)S(1)} %get-tuple-element.54.refs_9_.refs_14_) | copy-start | bytes 3145732
  27.2 5.0 %copy-start.11 = (bf16[8,256,256]{2,1,0:T(8,128)(2,1)}, bf16[8,256,256]{2,1,0:T(8,128)(2,1)S(1)}, u32[]{:S(2)}) copy-start(bf16[8,256,256]{2,1,0:T(8,128)(2,1)S(1)} %get-tuple-element.55.refs_10_.refs_15_) | copy-start | bytes 3145732
  27.2 5.0 %copy-start.17 = (bf16[8,256,256]{2,1,0:T(8,128)(2,1)}, bf16[8,256,256]{2,1,0:T(8,128)(2,1)S(1)}, u32[]{:S(2)}) copy-start(bf16[8,256,256]{2,1,0:T(8,128)(2,1)S(1)} %get-tuple-element.70.refs_16_) | copy-start | bytes 3145732
  27.2 5.0 %copy-start.41 = (f32[256,256]{1,0:T(8,128)}, f32[256,256]{1,0:T(8,128)S(1)}, u32[]{:S(2)}) copy-start(f32[256,256]{1,0:T(8,128)S(1)} %get-tuple-element.72.refs_0_) | copy-start | bytes 786436
  27.2 5.0 %copy-start.43 = (f32[256,256]{1,0:T(8,128)}, f32[256,256]{1,0:T(8,128)S(1)}, u32[]{:S(2)}) copy-start(f32[256,256]{1,0:T(8,128)S(1)} %get-tuple-element.73.refs_1_) | copy-start | bytes 786436
  27.2 5.0 %copy-start.45 = (f32[256,256]{1,0:T(8,128)}, f32[256,256]{1,0:T(8,128)S(1)}, u32[]{:S(2)}) copy-start(f32[256,256]{1,0:T(8,128)S(1)} %get-tuple-element.74.refs_2_) | copy-start | bytes 786436
  27.2 33.7 %collective-permute-start.6 = (f32[256,256]{1,0:T(8,128)}, f32[256,256]{1,0:T(8,128)}, u32[]{:S(2)}, u32[]{:S(2)}) collective-permute-start(f32[256,256]{1,0:T(8,128)} %get-tuple-element.60), channel_id=1, source_target_pairs={{0,128},{64,192},{128,0},{192,64},{1,129},{65,193},{129,1},{193,65... | collective-permute-start | bytes 786440 | tf_op jit(solution)/shard_map/ppermute | solution.py:382
  28.6 32.4 %collective-permute-start.7 = (f32[256,256]{1,0:T(8,128)}, f32[256,256]{1,0:T(8,128)}, u32[]{:S(2)}, u32[]{:S(2)}) collective-permute-start(f32[256,256]{1,0:T(8,128)} %get-tuple-element.61), channel_id=1, source_target_pairs={{0,192},{64,0},{128,64},{192,128},{1,193},{65,1},{129,65},{193,129... | collective-permute-start | bytes 786440 | tf_op jit(solution)/shard_map/ppermute | solution.py:382
  32.2 28.7 %collective-permute-start.10 = (f32[256,256]{1,0:T(8,128)}, f32[256,256]{1,0:T(8,128)}, u32[]{:S(2)}, u32[]{:S(2)}) collective-permute-start(f32[256,256]{1,0:T(8,128)} %get-tuple-element.62.refs_4_), channel_id=1, source_target_pairs={{0,192},{64,0},{128,64},{192,128},{1,193},{65,1},{129,65},{193,129... | collective-permute-start | bytes 786440 | tf_op jit(solution)/shard_map/ppermute | solution.py:382
  34.5 26.4 %collective-permute-start.9 = (f32[256,256]{1,0:T(8,128)}, f32[256,256]{1,0:T(8,128)}, u32[]{:S(2)}, u32[]{:S(2)}) collective-permute-start(f32[256,256]{1,0:T(8,128)} %get-tuple-element.62.refs_4_), channel_id=1, source_target_pairs={{0,128},{64,192},{128,0},{192,64},{1,129},{65,193},{129,1},{193,65... | collective-permute-start | bytes 786440 | tf_op jit(solution)/shard_map/ppermute | solution.py:382
  37.7 23.3 %collective-permute-start.8 = (f32[256,256]{1,0:T(8,128)}, f32[256,256]{1,0:T(8,128)}, u32[]{:S(2)}, u32[]{:S(2)}) collective-permute-start(f32[256,256]{1,0:T(8,128)} %get-tuple-element.62.refs_4_), channel_id=1, source_target_pairs={{0,64},{64,128},{128,192},{192,0},{1,65},{65,129},{129,193},{193,1... | collective-permute-start | bytes 786440 | tf_op jit(solution)/shard_map/ppermute | solution.py:382
  39.2 40.4 %all-to-all-start = ((f32[32,2,256]{2,1,0:T(2,128)}), f32[32,2,256]{2,1,0:T(2,128)S(1)}, u32[]{:S(2)}, u32[]{:S(2)}) async-start(f32[32,2,256]{2,1,0:T(2,128)} %get-tuple-element.56), calls=%async_computation | async-start | bytes 131072 | tf_op jit(solution)/shard_map/all_to_all | solution.py:458
  50.8 10.1 %copy-start.4 = (bf16[5,256,256]{2,1,0:T(8,128)(2,1)S(1)}, bf16[5,256,256]{2,1,0:T(8,128)(2,1)}, u32[]{:S(2)}) copy-start(bf16[5,256,256]{2,1,0:T(8,128)(2,1)} %copy-done.3) | copy-start | bytes 1966084
  138.5 13.7 %collective-permute-start.13 = (f32[8,40,256]{2,1,0:T(8,128)S(1)}, f32[8,40,256]{2,1,0:T(8,128)S(1)}, u32[]{:S(2)}, u32[]{:S(2)}) collective-permute-start(f32[8,40,256]{2,1,0:T(8,128)S(1)} %all_to_all.16.refs_1_), channel_id=1, source_target_pairs={{0,192},{64,0},{128,64},{192,128},{1,193},{65,1},{129,65},{193,129... | collective-permute-start | bytes 983048 | tf_op jit(solution)/shard_map/ppermute | solution.py:382
  139.3 12.9 %collective-permute-start.12 = (f32[8,40,256]{2,1,0:T(8,128)S(1)}, f32[8,40,256]{2,1,0:T(8,128)S(1)}, u32[]{:S(2)}, u32[]{:S(2)}) collective-permute-start(f32[8,40,256]{2,1,0:T(8,128)S(1)} %all_to_all.16.refs_1_), channel_id=1, source_target_pairs={{0,128},{64,192},{128,0},{192,64},{1,129},{65,193},{129,1},{193,65... | collective-permute-start | bytes 983048 | tf_op jit(solution)/shard_map/ppermute | solution.py:382
  140.4 12.4 %collective-permute-start.11 = (f32[8,40,256]{2,1,0:T(8,128)S(1)}, f32[8,40,256]{2,1,0:T(8,128)S(1)}, u32[]{:S(2)}, u32[]{:S(2)}) collective-permute-start(f32[8,40,256]{2,1,0:T(8,128)S(1)} %all_to_all.16.refs_1_), channel_id=1, source_target_pairs={{0,64},{64,128},{128,192},{192,0},{1,65},{65,129},{129,193},{193,1... | collective-permute-start | bytes 983048 | tf_op jit(solution)/shard_map/ppermute | solution.py:382
  (46 other events, 49.0 us)
